TPU v7x, 32 devices: a whole 2x2x4 slice. The times are simulated.
32 devices in a mesh: col: 8 (over z, x), row: 4 (over y, core).
Axes of the slice: x: 2, y: 2, z: 4, core: 2. Of those that a mesh axis runs over, the one named last changes fastest.
Arguments:
- right_side: float32 [8, 256, 256], P('col'), may hold values from -6 to 6
- coupling: bfloat16 [2, 4, 256, 81920], P(None, 'row', None, 'col'), may hold values from -0.01953125 to 0.01953125
- child_solution: bfloat16 [81920, 256], P(('col', 'row')), may hold values from -6 to 6
- factor_blocks: bfloat16 [2, 4, 256, 8, 256], P(None, 'row', None, 'col'), may hold values from -1 to 1
- pattern: int32 [8, 8], replicated, may hold values from 0 to 1, as said below
- diag_inverse: bfloat16 [8, 256, 256], P('col'), may hold values from -0.375 to 0.375
Outputs:
- solved: bfloat16 [8, 256, 256], P('col')
Inputs may be any that keep to these rules, and one draw needn't show every extreme that they name: pattern[j, j - 1] = 1 for every j from 1 to 7; entries with k >= j are not read.
All inputs are finite; a program needn't handle non-finite values.
Results may differ from a plain program's by a relative error of at most 0.017.
Values may be sent and summed in bfloat16 or wider, within the bound.
A program may use at most 64 MiB of HBM per device.

v0:
```python
import jax
import jax.numpy as jnp
from jax import lax
from jax.sharding import PartitionSpec as P


def per_device(right_side, coupling, child_solution, factor_blocks, pattern, diag_inverse):
    nrow = lax.axis_size("row")
    ncol = lax.axis_size("col")
    row_index = lax.axis_index("row")
    col_index = lax.axis_index("col")
    brows = coupling.shape[0]
    blk_size = coupling.shape[2]
    kcols = coupling.shape[3]
    rhs_count = child_solution.shape[1]
    nblk = pattern.shape[0]
    group = ncol // nblk
    part_rows = blk_size // group
    my_block = col_index // group
    my_offset = col_index % group * part_rows
    flat = coupling.reshape(brows * blk_size, kcols)
    update = jnp.dot(
        flat,
        lax.all_gather(child_solution, "row", axis=0, tiled=True),
        preferred_element_type=jnp.float32,
    )
    update = update.reshape(brows, blk_size, rhs_count)
    rhs_part = right_side.reshape(part_rows, rhs_count)
    placed = lax.dynamic_update_slice(
        jnp.zeros((blk_size, rhs_count), jnp.float32), rhs_part, (my_offset, jnp.int32(0))
    )
    blocks = factor_blocks.reshape(brows, blk_size, part_rows)
    inv_rows = diag_inverse.reshape(part_rows, blk_size)

    def advance(j, solved):
        j_row = j % nrow
        j_arow = j // nrow
        flags = lax.dynamic_index_in_dim(pattern, j, 0, keepdims=False)
        flag = lax.dynamic_index_in_dim(flags, my_block, 0, keepdims=False)
        keep = (flag > 0) & (my_block < j)
        masked = jnp.where(keep, solved, jnp.zeros_like(solved))
        row_blocks = lax.dynamic_index_in_dim(blocks, j_arow, 0, keepdims=False)
        partial_value = jnp.dot(row_blocks, masked, preferred_element_type=jnp.float32)
        partial_value = partial_value + lax.dynamic_index_in_dim(update, j_arow, 0, keepdims=False)
        partial_value = jnp.where(my_block == j, placed, jnp.zeros_like(placed)) - partial_value
        partial_value = jnp.where(row_index == j_row, partial_value, jnp.zeros_like(partial_value))
        total = lax.psum(partial_value, ("col", "row"))
        fresh = jnp.dot(
            inv_rows, total.astype(jnp.bfloat16), preferred_element_type=jnp.float32
        ).astype(jnp.bfloat16)
        return jnp.where(my_block == j, fresh, solved)

    start_state = jnp.zeros((part_rows, rhs_count), jnp.bfloat16)
    solved = lax.fori_loop(0, nblk, advance, start_state)
    return solved.reshape(1, part_rows, rhs_count)


def solution(mesh):
    in_specs = (
        P("col", None, None),
        P(None, "row", None, "col"),
        P(("col", "row"), None),
        P(None, "row", None, "col", None),
        P(),
        P("col", None, None),
    )
    out_specs = P("col", None, None)
    return jax.shard_map(
        per_device, mesh=mesh, in_specs=in_specs, out_specs=out_specs, check_vma=False
    )
```

profile of v0, /device:TPU:0, one launch (start us, length us, event | category | flops | bytes accessed | tf_op | source)
XLA Modules:
  0.0 424.0 jit_solution(1928758109962869587)
XLA Ops:
  6.5 0.0 all-gather.2.cloned.1.call-start
  6.5 0.7 all-gather.2.cloned.1.call-update
  7.3 1.1 copy.7
  8.4 0.0 copy-start
  8.4 0.0 copy-start.1
  8.4 43.7 %all-gather.2.cloned.1.call-done = bf16[10240,256]{1,0:T(8,128)(2,1)} async-done(((bf16[2560,256]{1,0:T(8,128)(2,1)}), bf16[10240,256]{1,0:T(8,128)(2,1)}) %all-gather.2.cloned.1.call-update) | async-done | bytes 5242896 | tf_op jit(solution)/shard_map/all_gather | solution.py:24
  52.1 8.4 %fusion.12 = f32[2,256,256]{1,2,0:T(8,128)S(1)} fusion(bf16[2,1,256,10240]{3,2,1,0:T(8,128)(2,1)} %param.9, bf16[10240,256]{1,0:T(8,128)(2,1)} %all-gather.2.cloned.1.call-done), kind=kOutput, calls=%fused_computation.15 | convolution fusion | flops 2684354560 | bytes 16252928 | tf_op jit(solution)/shard_map/dot_general | solution.py:22
  60.5 0.0 copy-done
  60.5 0.0 copy-done.1
  60.5 355.9 %while.17 = (s32[]{:T(128)}, bf16[256,256]{0,1:T(8,128)(2,1)S(1)}, s32[]{:T(128)}, s32[]{:T(128)}, f32[256,256]{0,1:T(8,128)S(1)}, /*index=5*/bf16[2,256,256]{2,...) while((s32[]{:T(128)}, bf16[256,256]{0,1:T(8,128)(2,1)S(1)}, ...), condition=%wide.region_2.3_spmd.clone, body=%wide.region_0.2_spmd.clone.sunk | while | flops 67764248 | bytes 1969544 | solution.py:54
  60.5 1.3 dynamic_slice.47
  62.5 0.2 fusion.27
  62.7 42.9 %all-reduce.1 = bf16[256,256]{0,1:T(8,128)(2,1)S(1)} all-reduce(f32[256,256]{0,1:T(8,128)S(1)} %fusion.27), channel_id=1, replica_groups=mesh['col'=8,'row'=4] {'col','row'}, use_global_device_ids=true, to_apply=%region_1.1 | all-reduce | flops 65536 | bytes 393216 | tf_op jit(solution)/shard_map/while/body/eval_jaxpr/psum | solution.py:47
  105.6 0.2 fusion.28
  105.9 1.3 dynamic_slice.47
  107.8 0.2 fusion.27
  108.0 41.9 %all-reduce.1 = bf16[256,256]{0,1:T(8,128)(2,1)S(1)} all-reduce(f32[256,256]{0,1:T(8,128)S(1)} %fusion.27), channel_id=1, replica_groups=mesh['col'=8,'row'=4] {'col','row'}, use_global_device_ids=true, to_apply=%region_1.1 | all-reduce | flops 65536 | bytes 393216 | tf_op jit(solution)/shard_map/while/body/eval_jaxpr/psum | solution.py:47
  150.0 0.2 fusion.28
  150.2 1.3 dynamic_slice.47
  152.2 0.2 fusion.27
  152.4 41.8 %all-reduce.1 = bf16[256,256]{0,1:T(8,128)(2,1)S(1)} all-reduce(f32[256,256]{0,1:T(8,128)S(1)} %fusion.27), channel_id=1, replica_groups=mesh['col'=8,'row'=4] {'col','row'}, use_global_device_ids=true, to_apply=%region_1.1 | all-reduce | flops 65536 | bytes 393216 | tf_op jit(solution)/shard_map/while/body/eval_jaxpr/psum | solution.py:47
  194.2 0.2 fusion.28
  194.5 1.3 dynamic_slice.47
  196.5 0.2 fusion.27
  196.7 41.9 %all-reduce.1 = bf16[256,256]{0,1:T(8,128)(2,1)S(1)} all-reduce(f32[256,256]{0,1:T(8,128)S(1)} %fusion.27), channel_id=1, replica_groups=mesh['col'=8,'row'=4] {'col','row'}, use_global_device_ids=true, to_apply=%region_1.1 | all-reduce | flops 65536 | bytes 393216 | tf_op jit(solution)/shard_map/while/body/eval_jaxpr/psum | solution.py:47
  238.6 0.2 fusion.28
  238.9 1.3 dynamic_slice.47
  240.9 0.2 fusion.27
  241.1 41.8 %all-reduce.1 = bf16[256,256]{0,1:T(8,128)(2,1)S(1)} all-reduce(f32[256,256]{0,1:T(8,128)S(1)} %fusion.27), channel_id=1, replica_groups=mesh['col'=8,'row'=4] {'col','row'}, use_global_device_ids=true, to_apply=%region_1.1 | all-reduce | flops 65536 | bytes 393216 | tf_op jit(solution)/shard_map/while/body/eval_jaxpr/psum | solution.py:47
  282.9 0.2 fusion.28
  283.1 1.3 dynamic_slice.47
  285.1 0.2 fusion.27
  285.3 42.0 %all-reduce.1 = bf16[256,256]{0,1:T(8,128)(2,1)S(1)} all-reduce(f32[256,256]{0,1:T(8,128)S(1)} %fusion.27), channel_id=1, replica_groups=mesh['col'=8,'row'=4] {'col','row'}, use_global_device_ids=true, to_apply=%region_1.1 | all-reduce | flops 65536 | bytes 393216 | tf_op jit(solution)/shard_map/while/body/eval_jaxpr/psum | solution.py:47
  327.3 0.2 fusion.28
  327.6 1.3 dynamic_slice.47
  329.5 0.2 fusion.27
  329.8 41.7 %all-reduce.1 = bf16[256,256]{0,1:T(8,128)(2,1)S(1)} all-reduce(f32[256,256]{0,1:T(8,128)S(1)} %fusion.27), channel_id=1, replica_groups=mesh['col'=8,'row'=4] {'col','row'}, use_global_device_ids=true, to_apply=%region_1.1 | all-reduce | flops 65536 | bytes 393216 | tf_op jit(solution)/shard_map/while/body/eval_jaxpr/psum | solution.py:47
  371.5 0.2 fusion.28
  371.7 1.3 dynamic_slice.47
  373.7 0.2 fusion.27
  373.9 42.2 %all-reduce.1 = bf16[256,256]{0,1:T(8,128)(2,1)S(1)} all-reduce(f32[256,256]{0,1:T(8,128)S(1)} %fusion.27), channel_id=1, replica_groups=mesh['col'=8,'row'=4] {'col','row'}, use_global_device_ids=true, to_apply=%region_1.1 | all-reduce | flops 65536 | bytes 393216 | tf_op jit(solution)/shard_map/while/body/eval_jaxpr/psum | solution.py:47
  416.1 0.2 fusion.28
  416.4 0.8 copy.9
  (1 shorter events, 0.0 us)
Async XLA Ops:
  6.5 45.5 %all-gather.2.cloned.1.call-start = ((), (), s32[]{:S(2)}) async-start(), calls=%async_computation | async-start | bytes 6553600 | tf_op jit(solution)/shard_map/all_gather | solution.py:24
  8.4 52.1 %copy-start = (bf16[2,1,256,1,256]{4,2,3,1,0:T(8,128)(2,1)S(1)}, bf16[2,1,256,1,256]{4,2,3,1,0:T(8,128)(2,1)}, u32[]{:S(2)}) copy-start(bf16[2,1,256,1,256]{4,2,3,1,0:T(8,128)(2,1)} %param.11) | copy-start | bytes 786436
  8.4 52.1 %copy-start.1 = (bf16[1,256,256]{2,1,0:T(8,128)(2,1)S(1)}, bf16[1,256,256]{2,1,0:T(8,128)(2,1)}, u32[]{:S(2)}) copy-start(bf16[1,256,256]{2,1,0:T(8,128)(2,1)} %param.13) | copy-start | bytes 393220
Sparse Core Ops, SparseCore 0:
  8.9 43.1 all-gather.1
where the time goes:
time: 425 us; the launch traced here: 424 us
  blocking collectives  336 us (79%)
  waiting for transfers between devices  44.4 us (10%)
  between operations  13.5 us (3%)
  local copies, waits for them, and re-layouts  12.3 us (3%)
  matrix products  12.1 us (3%)
  loops' own time  5.51 us (1%)
    psum x8, blocking collectives, advance(): total = lax.psum(partial_value, ('col', 'row'))  336 us
    all_gather x1, waiting for transfers between devices, per_device(): lax.all_gather(child_solution, 'row', axis=0, tiled=True)  43.7 us
    dynamic_slice x8, local copies, waits for them, and re-layouts, advance(): flag = lax.dynamic_index_in_dim(flags, my_block, 0, keepdims=False)  10.5 us
  transfers between devices with their start and end apart: 1, of which 1 were waited for; matrix products, arithmetic and copies ran while one was open for 0% of the time, Pallas kernels for 0%

commit v1 on v0

--- a/solution.py
+++ b/solution.py
@@ -44,7 +44,7 @@
         partial_value = partial_value + lax.dynamic_index_in_dim(update, j_arow, 0, keepdims=False)
         partial_value = jnp.where(my_block == j, placed, jnp.zeros_like(placed)) - partial_value
         partial_value = jnp.where(row_index == j_row, partial_value, jnp.zeros_like(partial_value))
-        total = lax.psum(partial_value, ("col", "row"))
+        total = jnp.sum(lax.all_gather(partial_value, ("col", "row")), axis=0)
         fresh = jnp.dot(
             inv_rows, total.astype(jnp.bfloat16), preferred_element_type=jnp.float32
         ).astype(jnp.bfloat16)

time: 425 us -> 740 us (1.74)
  waiting for transfers between devices: 44.4 us -> 661 us
  blocking collectives: 336 us -> 0 us
  other arithmetic: 0.01 us -> 31.3 us
    all_gather x0 -> x8, waiting for transfers between devices: none -> 615 us  [advance(): total = jnp.sum(lax.all_gather(partial_value, ('col', 'row')), axis=0)]
    psum x8 -> x0, blocking collectives: 336 us -> none  [advance(): total = lax.psum(partial_value, ('col', 'row'))]
    reduce_sum x0 -> x8, other arithmetic: none -> 31.3 us  [advance(): total = jnp.sum(lax.all_gather(partial_value, ('col', 'row')), axis=0)]
  transfers between devices with their start and end apart: 1 -> 9, of which waited for: 1 -> 9; matrix products, arithmetic and copies ran while one was open for 0% -> 0% of each run, Pallas kernels for 0% -> 0%
where the time goes in v1:
time: 740 us; the launch traced here: 739 us
  waiting for transfers between devices  661 us (89%)
  other arithmetic  31.3 us (4%)
  matrix products  16.1 us (2%)
  between operations  13.2 us (2%)
  local copies, waits for them, and re-layouts  11.4 us (2%)
    all_gather x8, waiting for transfers between devices, advance(): total = jnp.sum(lax.all_gather(partial_value, ('col', 'row')), axis=0)  615 us
    all_gather x1, waiting for transfers between devices, per_device(): lax.all_gather(child_solution, 'row', axis=0, tiled=True)  44.8 us
    reduce_sum x8, other arithmetic, advance(): total = jnp.sum(lax.all_gather(partial_value, ('col', 'row')), axis=0)  31.3 us
  transfers between devices with their start and end apart: 9, of which 9 were waited for; matrix products, arithmetic and copies ran while one was open for 0% of the time, Pallas kernels for 0%

profile of v1, /device:TPU:0, one launch (start us, length us, event | category | flops | bytes accessed | tf_op | source)
XLA Modules:
  0.0 739.2 jit_solution(12192096462909910116)
XLA Ops:
  6.5 0.7 all-gather.7.cloned.1.call-update
  7.3 0.0 copy-start
  7.3 0.0 copy-start.2
  7.3 0.0 copy-start.3
  7.3 44.8 %all-gather.7.cloned.1.call-done = bf16[10240,256]{1,0:T(8,128)(2,1)} async-done(((bf16[2560,256]{1,0:T(8,128)(2,1)}), bf16[10240,256]{1,0:T(8,128)(2,1)}) %all-gather.7.cloned.1.call-update) | async-done | bytes 5242896 | tf_op jit(solution)/shard_map/all_gather | solution.py:24
  52.1 7.1 fusion.12
  59.2 672.7 %while.17 = (s32[]{:T(128)}, bf16[256,256]{1,0:T(8,128)(2,1)S(1)}, s32[]{:T(128)}, s32[]{:T(128)}, f32[256,256]{1,0:T(8,128)S(1)}, /*index=5*/bf16[2,256,256]{2,...) while((s32[]{:T(128)}, bf16[256,256]{1,0:T(8,128)(2,1)S(1)}, ...), condition=%wide.region_2.3_spmd.clone, body=%wide.region_0.2_spmd.clone.sunk | while | flops 69730328 | bytes 36048312 | solution.py:54
  59.3 0.0 all-gather.9.cloned.1.call-start
  59.3 1.3 dynamic_slice.47
  61.4 0.9 fusion.27
  62.3 0.0 all-gather.9.cloned.1.call-update
  62.3 78.2 %all-gather.9.cloned.1.call-done = f32[8192,256]{1,0:T(8,128)} async-done(((f32[256,256]{1,0:T(8,128)}), f32[8192,256]{1,0:T(8,128)}) %all-gather.9.cloned.1.call-update) | async-done | bytes 8388624 | tf_op jit(solution)/shard_map/while/body/eval_jaxpr/all_gather | solution.py:47
  140.6 3.9 reduce_sum.19
  144.5 0.2 fusion.28
  144.7 0.0 all-gather.9.cloned.1.call-start
  144.8 1.3 dynamic_slice.47
  146.8 0.9 fusion.27
  147.8 0.0 all-gather.9.cloned.1.call-update
  147.8 76.8 %all-gather.9.cloned.1.call-done = f32[8192,256]{1,0:T(8,128)} async-done(((f32[256,256]{1,0:T(8,128)}), f32[8192,256]{1,0:T(8,128)}) %all-gather.9.cloned.1.call-update) | async-done | bytes 8388624 | tf_op jit(solution)/shard_map/while/body/eval_jaxpr/all_gather | solution.py:47
  224.6 3.9 reduce_sum.19
  228.5 0.2 fusion.28
  228.7 0.0 all-gather.9.cloned.1.call-start
  228.8 1.3 dynamic_slice.47
  230.9 0.9 fusion.27
  231.8 0.0 all-gather.9.cloned.1.call-update
  231.8 76.5 %all-gather.9.cloned.1.call-done = f32[8192,256]{1,0:T(8,128)} async-done(((f32[256,256]{1,0:T(8,128)}), f32[8192,256]{1,0:T(8,128)}) %all-gather.9.cloned.1.call-update) | async-done | bytes 8388624 | tf_op jit(solution)/shard_map/while/body/eval_jaxpr/all_gather | solution.py:47
  308.3 3.9 reduce_sum.19
  312.2 0.2 fusion.28
  312.4 0.0 all-gather.9.cloned.1.call-start
  312.5 1.3 dynamic_slice.47
  314.6 0.9 fusion.27
  315.5 0.0 all-gather.9.cloned.1.call-update
  315.5 76.5 %all-gather.9.cloned.1.call-done = f32[8192,256]{1,0:T(8,128)} async-done(((f32[256,256]{1,0:T(8,128)}), f32[8192,256]{1,0:T(8,128)}) %all-gather.9.cloned.1.call-update) | async-done | bytes 8388624 | tf_op jit(solution)/shard_map/while/body/eval_jaxpr/all_gather | solution.py:47
  392.0 3.9 reduce_sum.19
  395.9 0.2 fusion.28
  396.2 0.0 all-gather.9.cloned.1.call-start
  396.3 1.3 dynamic_slice.47
  398.3 0.9 fusion.27
  399.2 0.0 all-gather.9.cloned.1.call-update
  399.2 76.5 %all-gather.9.cloned.1.call-done = f32[8192,256]{1,0:T(8,128)} async-done(((f32[256,256]{1,0:T(8,128)}), f32[8192,256]{1,0:T(8,128)}) %all-gather.9.cloned.1.call-update) | async-done | bytes 8388624 | tf_op jit(solution)/shard_map/while/body/eval_jaxpr/all_gather | solution.py:47
  475.7 3.9 reduce_sum.19
  479.7 0.2 fusion.28
  479.9 0.0 all-gather.9.cloned.1.call-start
  480.0 1.3 dynamic_slice.47
  482.0 0.9 fusion.27
  482.9 0.0 all-gather.9.cloned.1.call-update
  483.0 76.8 %all-gather.9.cloned.1.call-done = f32[8192,256]{1,0:T(8,128)} async-done(((f32[256,256]{1,0:T(8,128)}), f32[8192,256]{1,0:T(8,128)}) %all-gather.9.cloned.1.call-update) | async-done | bytes 8388624 | tf_op jit(solution)/shard_map/while/body/eval_jaxpr/all_gather | solution.py:47
  559.8 3.9 reduce_sum.19
  563.7 0.2 fusion.28
  563.9 0.0 all-gather.9.cloned.1.call-start
  564.0 1.3 dynamic_slice.47
  566.0 0.9 fusion.27
  567.0 0.0 all-gather.9.cloned.1.call-update
  567.0 76.8 %all-gather.9.cloned.1.call-done = f32[8192,256]{1,0:T(8,128)} async-done(((f32[256,256]{1,0:T(8,128)}), f32[8192,256]{1,0:T(8,128)}) %all-gather.9.cloned.1.call-update) | async-done | bytes 8388624 | tf_op jit(solution)/shard_map/while/body/eval_jaxpr/all_gather | solution.py:47
  643.8 3.9 reduce_sum.19
  647.7 0.2 fusion.28
  647.9 0.0 all-gather.9.cloned.1.call-start
  648.0 1.3 dynamic_slice.47
  650.1 0.9 fusion.27
  651.0 0.0 all-gather.9.cloned.1.call-update
  651.0 76.8 %all-gather.9.cloned.1.call-done = f32[8192,256]{1,0:T(8,128)} async-done(((f32[256,256]{1,0:T(8,128)}), f32[8192,256]{1,0:T(8,128)}) %all-gather.9.cloned.1.call-update) | async-done | bytes 8388624 | tf_op jit(solution)/shard_map/while/body/eval_jaxpr/all_gather | solution.py:47
  727.8 3.9 reduce_sum.19
  731.8 0.2 fusion.28
  732.0 0.6 copy-done.1
  (6 shorter events, 0.0 us)
Async XLA Ops:
  6.5 45.5 %all-gather.7.cloned.1.call-start = ((), (), s32[]{:S(2)}) async-start(), calls=%async_computation | async-start | bytes 6553600 | tf_op jit(solution)/shard_map/all_gather | solution.py:24
  7.3 51.9 %copy-start = (f32[1,256,256]{2,1,0:T(8,128)S(1)}, f32[1,256,256]{2,1,0:T(8,128)}, u32[]{:S(2)}) copy-start(f32[1,256,256]{2,1,0:T(8,128)} %param.8) | copy-start | bytes 786436
  7.3 51.9 %copy-start.2 = (bf16[2,1,256,1,256]{4,2,3,1,0:T(8,128)(2,1)S(1)}, bf16[2,1,256,1,256]{4,2,3,1,0:T(8,128)(2,1)}, u32[]{:S(2)}) copy-start(bf16[2,1,256,1,256]{4,2,3,1,0:T(8,128)(2,1)} %param.11) | copy-start | bytes 786436
  7.3 51.9 %copy-start.3 = (bf16[1,256,256]{2,1,0:T(8,128)(2,1)S(1)}, bf16[1,256,256]{2,1,0:T(8,128)(2,1)}, u32[]{:S(2)}) copy-start(bf16[1,256,256]{2,1,0:T(8,128)(2,1)} %param.13) | copy-start | bytes 393220
  59.3 81.3 %all-gather.9.cloned.1.call-start = ((), (), s32[]{:S(2)}) async-start(), calls=%async_computation.1 | async-start | bytes 8650752 | tf_op jit(solution)/shard_map/while/body/eval_jaxpr/all_gather | solution.py:47
  144.7 79.9 %all-gather.9.cloned.1.call-start = ((), (), s32[]{:S(2)}) async-start(), calls=%async_computation.1 | async-start | bytes 8650752 | tf_op jit(solution)/shard_map/while/body/eval_jaxpr/all_gather | solution.py:47
  228.7 79.6 %all-gather.9.cloned.1.call-start = ((), (), s32[]{:S(2)}) async-start(), calls=%async_computation.1 | async-start | bytes 8650752 | tf_op jit(solution)/shard_map/while/body/eval_jaxpr/all_gather | solution.py:47
  312.4 79.6 %all-gather.9.cloned.1.call-start = ((), (), s32[]{:S(2)}) async-start(), calls=%async_computation.1 | async-start | bytes 8650752 | tf_op jit(solution)/shard_map/while/body/eval_jaxpr/all_gather | solution.py:47
  396.2 79.6 %all-gather.9.cloned.1.call-start = ((), (), s32[]{:S(2)}) async-start(), calls=%async_computation.1 | async-start | bytes 8650752 | tf_op jit(solution)/shard_map/while/body/eval_jaxpr/all_gather | solution.py:47
  479.9 79.9 %all-gather.9.cloned.1.call-start = ((), (), s32[]{:S(2)}) async-start(), calls=%async_computation.1 | async-start | bytes 8650752 | tf_op jit(solution)/shard_map/while/body/eval_jaxpr/all_gather | solution.py:47
  563.9 79.9 %all-gather.9.cloned.1.call-start = ((), (), s32[]{:S(2)}) async-start(), calls=%async_computation.1 | async-start | bytes 8650752 | tf_op jit(solution)/shard_map/while/body/eval_jaxpr/all_gather | solution.py:47
  647.9 79.9 %all-gather.9.cloned.1.call-start = ((), (), s32[]{:S(2)}) async-start(), calls=%async_computation.1 | async-start | bytes 8650752 | tf_op jit(solution)/shard_map/while/body/eval_jaxpr/all_gather | solution.py:47
  732.0 0.7 copy-start.1
Sparse Core Ops, SparseCore 0:
  8.9 43.1 all-gather.6
  63.0 77.5 all-gather.8
  148.4 76.1 all-gather.8
  232.1 76.1 all-gather.8
  315.8 76.1 all-gather.8
  399.6 76.1 all-gather.8
  483.6 76.1 all-gather.8
  567.6 76.1 all-gather.8
  651.7 76.1 all-gather.8
